TPU v7x, 256 devices: a whole 4x4x8 slice. The times are simulated.
256 devices in a mesh: chol: 8 (over z), vol: 32 (over y, x, core).
Axes of the slice: x: 4, y: 4, z: 8, core: 2. Of those that a mesh axis runs over, the one named last changes fastest.
Arguments:
- diag_block: float32 [1024, 1024], P('vol'), as said below
- rhs_diag: float32 [3, 1024], P(None, 'vol'), may hold values from -0.3125 to 0.3125
- panel_block: float32 [32768, 1024], P(('chol', 'vol')), may hold values from -0.625 to 0.625
- rhs_panel: float32 [3, 32768], P(None, ('chol', 'vol')), may hold values from -1.25 to 1.25
- trail: float32 [32768, 1024], P(('chol', 'vol')), may hold values from -6 to 6
- ctrl_xyz: float32 [3, 32768], P(None, ('chol', 'vol')), may hold values from 0 to 256, as said below
- node_xyz: float32 [3, 2097152], P(None, ('chol', 'vol')), may hold values from 0 to 256, as said below
- tile_blocks: int32 [16384, 8], P(('chol', 'vol')), may hold values from 0 to 255, as said below
- tile_count: int32 [16384], P(('chol', 'vol')), may hold values from 3 to 8, as said below
- face_area: float32 [3, 6, 2097152], P(None, None, ('chol', 'vol')), may hold values from -1.25 to 1.25
- edge_nbr: int32 [6, 2097152], P(None, ('chol', 'vol')), may hold values from 0 to 8447, as said below
- old_volume: float32 [2097152], P(('chol', 'vol')), may hold values from 0.5 to 2
Outputs:
- trail_out: float32 [32768, 1024], P(('chol', 'vol'))
- node_disp: float32 [3, 2097152], P(None, ('chol', 'vol'))
- new_volume: float32 [2097152], P(('chol', 'vol'))
Inputs may be any that keep to these rules, and one draw needn't show every extreme that they name: diag_block is symmetric and each diagonal entry exceeds the sum of magnitudes of the other entries of its row by 0.05 or more. tile_count gives how many leading slots of a tile's list are used. `tile_blocks`: the used slots of a tile name consecutive control blocks in increasing order; the unused ones repeat its first block. `ctrl_xyz`: the first coordinate of control point j lies in [j // 128, j // 128 + 1). `node_xyz`: the first coordinate is a position along the hull in units of one control block's length. For node n at position p of its partition, edge_nbr[e, n] - p - 128 is a nonzero offset of at most 128 in magnitude.
All inputs are finite; a program needn't handle non-finite values.
Results may differ from a plain program's by a relative error of at most 0.0003.
Values sent between devices are 32-bit elements; how exact they have to be, the bound alone decides.
No kernel may reach another device: no remote copies, remote signals or barrier semaphores. Data moves between devices by JAX's collectives and lax.ppermute only.
A program may use at most 128 MiB of HBM per device.

v0:
```python
import jax
import jax.numpy as jnp
from jax import lax
from jax.sharding import PartitionSpec as P

HALO = 128
highest_mode = lax.Precision.HIGHEST
support_radius = 1.25


def with_halo(block, sides, width):
    for axis, dim in sides:
        count = lax.axis_size(axis)
        forward = [(i, i + 1) for i in range(count - 1)]
        backward = [(target, source) for source, target in forward]
        low = lax.ppermute(
            lax.slice_in_dim(block, block.shape[dim] - width, None, axis=dim), axis, forward
        )
        high = lax.ppermute(lax.slice_in_dim(block, 0, width, axis=dim), axis, backward)
        block = jnp.concatenate([low, block, high], axis=dim)
    return block


def wendland(dist_sq):
    scaled = jnp.sqrt(dist_sq) / support_radius
    remain = jnp.maximum(1.0 - scaled, 0.0)
    return remain**4 * (4.0 * scaled + 1.0)


def slot_term(tile_xyz, chosen, live_mask, blocks_xyz, blocks_weight):
    near_xyz = blocks_xyz[:, chosen]
    near_weight = blocks_weight[:, chosen]
    dist_sq = jnp.zeros((tile_xyz.shape[1], 128, 128), jnp.float32)
    for axis_pos in range(3):
        differ = tile_xyz[axis_pos][:, :, None] - near_xyz[axis_pos][:, None, :]
        dist_sq = dist_sq + differ * differ
    kernel = wendland(dist_sq)
    term = jnp.einsum("tnc,atc->atn", kernel, near_weight, precision=highest_mode)
    return term * live_mask[None, :, None]


def per_device(
    diag_block,
    rhs_diag,
    panel_block,
    rhs_panel,
    trail,
    ctrl_xyz,
    node_xyz,
    tile_blocks,
    tile_count,
    face_area,
    edge_nbr,
    old_volume,
):
    whole_diag, whole_rhs = (
        lax.all_gather(diag_block, "vol", axis=0, tiled=True),
        lax.all_gather(rhs_diag, "vol", axis=1, tiled=True),
    )
    factor = jnp.linalg.cholesky(whole_diag)
    lower_panel = jax.scipy.linalg.solve_triangular(factor, panel_block.T, lower=True).T
    forward = jax.scipy.linalg.solve_triangular(factor, whole_rhs.T, lower=True)
    ctrl_weight = rhs_panel - jnp.dot(lower_panel, forward, precision=highest_mode).T
    gathered_xyz, gathered_weight = (
        lax.all_gather(ctrl_xyz, ("chol", "vol"), axis=1, tiled=True),
        lax.all_gather(ctrl_weight, ("chol", "vol"), axis=1, tiled=True),
    )
    products = jnp.dot(
        lower_panel,
        lax.all_gather(lower_panel, "chol", axis=0, tiled=True).T,
        precision=highest_mode,
    )
    trail_out = trail - products
    blocks_xyz = gathered_xyz.reshape(3, -1, 128)
    blocks_weight = gathered_weight.reshape(3, -1, 128)
    tile_xyz = node_xyz.reshape(3, -1, 128)
    tile_total = tile_xyz.shape[1]
    zeros_start = jnp.zeros((3, tile_total, 128), jnp.float32)
    running = zeros_start
    for slot_index in range(tile_blocks.shape[1]):
        live_mask = (slot_index < tile_count).astype(jnp.float32)
        running = running + slot_term(
            tile_xyz, tile_blocks[:, slot_index], live_mask, blocks_xyz, blocks_weight
        )
    node_disp = running.reshape(3, -1)
    extended = with_halo(node_disp, (("vol", 1),), HALO)
    across_disp = extended[:, edge_nbr]
    flux = jnp.sum(face_area * (node_disp[:, None, :] + across_disp), axis=(0, 1))
    new_volume = old_volume + 0.5 * flux
    return (trail_out, node_disp, new_volume)


def solution(mesh):
    return jax.shard_map(
        per_device,
        mesh=mesh,
        in_specs=(
            P("vol", None),
            P(None, "vol"),
            P(("chol", "vol"), None),
            P(None, ("chol", "vol")),
            P(("chol", "vol"), None),
            P(None, ("chol", "vol")),
            P(None, ("chol", "vol")),
            P(("chol", "vol"), None),
            P(("chol", "vol")),
            P(None, None, ("chol", "vol")),
            P(None, ("chol", "vol")),
            P(("chol", "vol")),
        ),
        out_specs=(P(("chol", "vol"), None), P(None, ("chol", "vol")), P(("chol", "vol"))),
        check_vma=False,
    )
```

profile of v0, /device:TPU:7, one launch (start us, length us, event | category | flops | bytes accessed | tf_op | source)
XLA Modules:
  0.0 815.5 jit_solution(8358613724519774428)
XLA Ops:
  8.0 24.6 %all-gather = f32[32,32,3]{1,2,0:T(4,128)S(1)} all-gather(f32[1,32,3]{1,2,0:T(4,128)} %bitcast.337), channel_id=1, replica_groups=mesh['chol'=8,'vol'=32] {'vol'}, dimensions={0}, use_global_device_ids=true | all-gather | bytes 12672 | tf_op jit(solution)/shard_map/all_gather | solution.py:58
  34.4 1.2 copy.43
  36.7 69.3 %all_gather.19 = f32[3,32768]{1,0:T(4,128)S(1)} all-gather(f32[3,128]{1,0:T(4,128)} %param.17), channel_id=1, replica_groups=mesh['chol'=8,'vol'=32] {'chol','vol'}, dimensions={1}, use_global_device_ids=true | all-gather | bytes 394752 | tf_op jit(solution)/shard_map/all_gather | solution.py:65
  112.0 5.5 copy.42
  117.6 4.4 fusion
  122.0 1.9 copy-done.1
  124.0 11.7 %cholesky.223 = f32[128,128]{1,0:T(8,128)S(1)} custom-call(f32[128,128]{1,0:T(8,128)S(1)} %cholesky.580), custom_call_target="Cholesky" | custom-call | tf_op jit(solution)/shard_map/jit(cholesky)/cholesky | solution.py:60
  135.7 9.8 %custom-call.66 = f32[1,128,128]{1,2,0:T(8,128)S(1)} custom-call(f32[1,128,128]{2,1,0:T(8,128)S(1)} %get-tuple-element.107), custom_call_target="InvertDiagBlocksLowerTriangular" | custom-call | tf_op jit(solution)/shard_map/jit(cholesky)/cholesky | solution.py:60
  145.6 2.5 cholesky.255
  148.1 2.4 constant_dynamic-update-slice_fusion.57
  150.4 1.5 convolution_subtract_fusion.1
  152.0 11.9 %cholesky.244 = f32[128,128]{1,0:T(8,128)S(1)} custom-call(f32[128,128]{1,0:T(8,128)S(1)} %cholesky.584), custom_call_target="Cholesky" | custom-call | tf_op jit(solution)/shard_map/jit(cholesky)/cholesky | solution.py:60
  164.5 9.8 %custom-call.67 = f32[1,128,128]{1,2,0:T(8,128)S(1)} custom-call(f32[1,128,128]{2,1,0:T(8,128)S(1)} %get-tuple-element.104), custom_call_target="InvertDiagBlocksLowerTriangular" | custom-call | tf_op jit(solution)/shard_map/jit(cholesky)/cholesky | solution.py:60
  174.3 1.3 convolution_dynamic-update-slice_fusion
  175.6 2.1 convolution_subtract_fusion.2
  177.7 11.7 %cholesky.468 = f32[128,128]{1,0:T(8,128)S(1)} custom-call(f32[128,128]{1,0:T(8,128)S(1)} %cholesky.589), custom_call_target="Cholesky" | custom-call | tf_op jit(solution)/shard_map/jit(cholesky)/cholesky | solution.py:60
  190.7 9.8 %custom-call.68 = f32[1,128,128]{1,2,0:T(8,128)S(1)} custom-call(f32[1,128,128]{2,1,0:T(8,128)S(1)} %get-tuple-element.101), custom_call_target="InvertDiagBlocksLowerTriangular" | custom-call | tf_op jit(solution)/shard_map/jit(cholesky)/cholesky | solution.py:60
  200.5 1.2 convolution_dynamic-update-slice_fusion.1
  201.7 2.3 convolution_subtract_fusion.3
  204.1 12.1 %cholesky.487 = f32[128,128]{1,0:T(8,128)S(1)} custom-call(f32[128,128]{1,0:T(8,128)S(1)} %cholesky.594), custom_call_target="Cholesky" | custom-call | tf_op jit(solution)/shard_map/jit(cholesky)/cholesky | solution.py:60
  217.5 9.8 %custom-call.69 = f32[1,128,128]{1,2,0:T(8,128)S(1)} custom-call(f32[1,128,128]{2,1,0:T(8,128)S(1)} %get-tuple-element.98), custom_call_target="InvertDiagBlocksLowerTriangular" | custom-call | tf_op jit(solution)/shard_map/jit(cholesky)/cholesky | solution.py:60
  228.4 2.3 convolution_subtract_fusion.4
  230.8 11.7 %cholesky.506 = f32[128,128]{1,0:T(8,128)S(1)} custom-call(f32[128,128]{1,0:T(8,128)S(1)} %cholesky.599), custom_call_target="Cholesky" | custom-call | tf_op jit(solution)/shard_map/jit(cholesky)/cholesky | solution.py:60
  243.9 9.9 %custom-call.70 = f32[1,128,128]{1,2,0:T(8,128)S(1)} custom-call(f32[1,128,128]{2,1,0:T(8,128)S(1)} %get-tuple-element.95), custom_call_target="InvertDiagBlocksLowerTriangular" | custom-call | tf_op jit(solution)/shard_map/jit(cholesky)/cholesky | solution.py:60
  254.8 2.3 convolution_subtract_fusion.5
  257.1 11.7 %cholesky.526 = f32[128,128]{1,0:T(8,128)S(1)} custom-call(f32[128,128]{1,0:T(8,128)S(1)} %cholesky.604), custom_call_target="Cholesky" | custom-call | tf_op jit(solution)/shard_map/jit(cholesky)/cholesky | solution.py:60
  270.1 9.8 %custom-call.71 = f32[1,128,128]{1,2,0:T(8,128)S(1)} custom-call(f32[1,128,128]{2,1,0:T(8,128)S(1)} %get-tuple-element.92), custom_call_target="InvertDiagBlocksLowerTriangular" | custom-call | tf_op jit(solution)/shard_map/jit(cholesky)/cholesky | solution.py:60
  280.8 2.0 convolution_subtract_fusion.6
  282.9 11.9 %cholesky.546 = f32[128,128]{1,0:T(8,128)S(1)} custom-call(f32[128,128]{1,0:T(8,128)S(1)} %cholesky.609), custom_call_target="Cholesky" | custom-call | tf_op jit(solution)/shard_map/jit(cholesky)/cholesky | solution.py:60
  296.1 9.8 %custom-call.72 = f32[1,128,128]{1,2,0:T(8,128)S(1)} custom-call(f32[1,128,128]{2,1,0:T(8,128)S(1)} %get-tuple-element.89), custom_call_target="InvertDiagBlocksLowerTriangular" | custom-call | tf_op jit(solution)/shard_map/jit(cholesky)/cholesky | solution.py:60
  306.7 1.9 convolution_subtract_fusion.12
  308.6 11.7 %cholesky.564 = f32[128,128]{1,0:T(8,128)S(1)} custom-call(f32[128,128]{1,0:T(8,128)S(1)} %convolution_subtract_fusion.12), custom_call_target="Cholesky" | custom-call | tf_op jit(solution)/shard_map/jit(cholesky)/cholesky | solution.py:60
  327.3 4.8 select_select_fusion
  332.1 27.6 %while.1 = (s32[]{:T(128)}, f32[1024,1024]{1,0:T(8,128)}, s32[8,2]{0,1:T(2,128)S(1)}, f32[8,128,128]{2,1,0:T(8,128)}, s32[]{:T(128)}) while((s32[]{:T(128)}, f32[1024,1024]{1,0:T(8,128)}, s32[8,2]{0,1:T(2,128)S(1)}, f32[8,128,128]{2,1,0:T(8,128)}, s32[]{:T(128)}) %tuple.128), condition=%wide.while_cond, body=%wide.while_body.sunk | while | flops 2 | bytes 132205 | solution.py:61
  332.7 2.9 bitcast_dynamic-update-slice_fusion.2
  336.2 2.9 bitcast_dynamic-update-slice_fusion.2
  339.6 2.9 bitcast_dynamic-update-slice_fusion.2
  343.1 2.9 bitcast_dynamic-update-slice_fusion.2
  346.5 2.9 bitcast_dynamic-update-slice_fusion.2
  350.0 2.9 bitcast_dynamic-update-slice_fusion.2
  353.4 2.9 bitcast_dynamic-update-slice_fusion.2
  356.9 2.8 bitcast_dynamic-update-slice_fusion.2
  359.7 79.8 %custom-call.73 = f32[8,128,128]{1,2,0:T(8,128)S(1)} custom-call(f32[8,128,128]{2,1,0:T(8,128)} %get-tuple-element.10), custom_call_target="InvertDiagBlocksLowerTriangular" | custom-call | tf_op jit(solution)/shard_map/jit(_solve_triangular)/triangular_solve | solution.py:61
  440.0 1.3 convolution_subtract_fusion.11
  441.5 1.2 convolution_subtract_fusion.10
  443.0 1.2 convolution_subtract_fusion.14
  444.6 1.3 convolution_subtract_fusion.13
  446.2 1.4 convolution_subtract_fusion.9
  453.8 65.6 %all_gather.18 = f32[3,32768]{1,0:T(4,128)S(1)} all-gather(f32[3,128]{1,0:T(4,128)S(1)} %convolution_subtract_fusion.21), channel_id=1, replica_groups=mesh['chol'=8,'vol'=32] {'chol','vol'}, dimensions={1}, use_global_device_ids=true | all-gather | bytes 394752 | tf_op jit(solution)/shard_map/all_gather | solution.py:66
  524.7 10.7 %fusion.231 = f32[64,3,128]{2,1,0:T(4,128)S(1)} fusion(f32[64,128]{1,0:T(8,128)S(1)} %bitcast.336, f32[64,128]{1,0:T(8,128)S(1)} %bitcast.335, f32[64,128]{1,0:T(8,128)S(1)} %bitcast.334, f32[64,128]{1,0:T(8,128)S(1)} %bitcast.306, f32[64,128]{1,0:T(8,128)S(1)} %bitcast.314, f32[64,128]{1,0:T(8,128)S(1)} %bitcast.298, f32[64,3,128]{2,1,0:T(4,128)S(1)} %gather_fusion.2, ...), kind=kOutput, calls=%fused_computation.261 | convolution fusion | flops 54550528 | bytes 393472 | tf_op jit(solution)/shard_map/tnc,atc->atn/dot_general | solution.py:38
  535.4 10.5 %fusion.228 = f32[64,3,128]{2,1,0:T(4,128)S(1)} fusion(f32[64,3,128]{2,1,0:T(4,128)S(1)} %fusion.231, f32[64,128]{1,0:T(8,128)S(1)} %bitcast.333, f32[64,128]{1,0:T(8,128)S(1)} %bitcast.307, f32[64,128]{1,0:T(8,128)S(1)} %bitcast.332, f32[64,128]{1,0:T(8,128)S(1)} %bitcast.315, f32[64,128]{1,0:T(8,128)S(1)} %bitcast.331, f32[64,128]{1,0:T(8,128)S(1)} %bitcast.299, ...), kind=kOutput, calls=%fused_computation.260 | convolution fusion | flops 54575104 | bytes 491776 | tf_op jit(solution)/shard_map/tnc,atc->atn/dot_general | solution.py:38
  545.9 10.5 %fusion.237 = f32[64,3,128]{2,1,0:T(4,128)S(1)} fusion(f32[64,3,128]{2,1,0:T(4,128)S(1)} %fusion.228, f32[64,128]{1,0:T(8,128)S(1)} %bitcast.330, f32[64,128]{1,0:T(8,128)S(1)} %bitcast.329, f32[64,128]{1,0:T(8,128)S(1)} %bitcast.328, f32[64,128]{1,0:T(8,128)S(1)} %bitcast.308, f32[64,128]{1,0:T(8,128)S(1)} %bitcast.316, f32[64,128]{1,0:T(8,128)S(1)} %bitcast.300, ...), kind=kOutput, calls=%fused_computation.263 | convolution fusion | flops 54575104 | bytes 491776 | tf_op jit(solution)/shard_map/tnc,atc->atn/dot_general | solution.py:38
  556.4 10.5 %fusion.243 = f32[64,3,128]{2,1,0:T(4,128)S(1)} fusion(f32[64,3,128]{2,1,0:T(4,128)S(1)} %fusion.237, f32[64,128]{1,0:T(8,128)S(1)} %bitcast.327, f32[64,128]{1,0:T(8,128)S(1)} %bitcast.326, f32[64,128]{1,0:T(8,128)S(1)} %bitcast.325, f32[64,128]{1,0:T(8,128)S(1)} %bitcast.309, f32[64,128]{1,0:T(8,128)S(1)} %bitcast.317, f32[64,128]{1,0:T(8,128)S(1)} %bitcast.301, ...), kind=kOutput, calls=%fused_computation.265 | convolution fusion | flops 54575104 | bytes 491776 | tf_op jit(solution)/shard_map/tnc,atc->atn/dot_general | solution.py:38
  566.9 10.5 %fusion.249 = f32[64,3,128]{2,1,0:T(4,128)S(1)} fusion(f32[64,3,128]{2,1,0:T(4,128)S(1)} %fusion.243, f32[64,128]{1,0:T(8,128)S(1)} %bitcast.324, f32[64,128]{1,0:T(8,128)S(1)} %bitcast.323, f32[64,128]{1,0:T(8,128)S(1)} %bitcast.322, f32[64,128]{1,0:T(8,128)S(1)} %bitcast.310, f32[64,128]{1,0:T(8,128)S(1)} %bitcast.318, f32[64,128]{1,0:T(8,128)S(1)} %bitcast.302, ...), kind=kOutput, calls=%fused_computation.267 | convolution fusion | flops 54575104 | bytes 491776 | tf_op jit(solution)/shard_map/tnc,atc->atn/dot_general | solution.py:38
  577.4 10.5 %fusion.255 = f32[64,3,128]{2,1,0:T(4,128)S(1)} fusion(f32[64,3,128]{2,1,0:T(4,128)S(1)} %fusion.249, f32[64,128]{1,0:T(8,128)S(1)} %bitcast.297, f32[64,128]{1,0:T(8,128)S(1)} %bitcast.296, f32[64,128]{1,0:T(8,128)S(1)} %bitcast.295, f32[64,128]{1,0:T(8,128)S(1)} %bitcast.311, f32[64,128]{1,0:T(8,128)S(1)} %bitcast.319, f32[64,128]{1,0:T(8,128)S(1)} %bitcast.303, ...), kind=kOutput, calls=%fused_computation.269 | convolution fusion | flops 54575104 | bytes 491776 | tf_op jit(solution)/shard_map/tnc,atc->atn/dot_general | solution.py:38
  587.9 10.5 %fusion.261 = f32[64,3,128]{2,1,0:T(4,128)S(1)} fusion(f32[64,3,128]{2,1,0:T(4,128)S(1)} %fusion.255, f32[64,128]{1,0:T(8,128)S(1)} %bitcast.294, f32[64,128]{1,0:T(8,128)S(1)} %bitcast.293, f32[64,128]{1,0:T(8,128)S(1)} %bitcast.292, f32[64,128]{1,0:T(8,128)S(1)} %bitcast.312, f32[64,128]{1,0:T(8,128)S(1)} %bitcast.320, f32[64,128]{1,0:T(8,128)S(1)} %bitcast.304, ...), kind=kOutput, calls=%fused_computation.271 | convolution fusion | flops 54575104 | bytes 491776 | tf_op jit(solution)/shard_map/tnc,atc->atn/dot_general | solution.py:38
  598.5 10.5 %fusion.270 = f32[3,8192]{1,0:T(4,128)S(1)} fusion(f32[64,3,128]{2,1,0:T(4,128)S(1)} %fusion.261, f32[64,128]{1,0:T(8,128)S(1)} %bitcast.291, f32[64,128]{1,0:T(8,128)S(1)} %bitcast.290, f32[64,128]{1,0:T(8,128)S(1)} %bitcast.289, f32[64,128]{1,0:T(8,128)S(1)} %bitcast.313, f32[64,128]{1,0:T(8,128)S(1)} %bitcast.321, f32[64,128]{1,0:T(8,128)S(1)} %bitcast.305, ...), kind=kOutput, calls=%fused_computation.274 | convolution fusion | flops 54575104 | bytes 491776 | tf_op jit(solution)/shard_map/tnc,atc->atn/dot_general | solution.py:38
  609.0 3.5 collective-permute-start
  612.4 1.9 collective-permute-start.1
  614.4 5.0 collective-permute-done.1
  619.5 2.7 copy.60
  622.2 164.1 %gather_fusion.16 = f32[49152,3]{1,0:T(8,128)} fusion(f32[3,8448]{0,1:T(8,128)} %copy.60, s32[49152]{0:T(1024)S(1)} %broadcast_clamp_fusion), kind=kCustom, calls=%fused_computation.16 | custom fusion | bytes 1376256 | tf_op jit(solution)/shard_map/gather | solution.py:87
  786.4 15.9 %copy.61 = f32[6,8192,3]{1,0,2:T(8,128)S(1)} copy(f32[6,8192,3]{2,1,0:T(8,128)} %bitcast.255) | data formatting | bytes 1179648 | tf_op jit(solution)/shard_map/gather | solution.py:87
  803.1 5.4 convolution_subtract_fusion
  (154 shorter events, 41.3 us)
Async XLA Ops:
  7.2 104.1 %copy-start.10 = (s32[64]{0:T(128)S(1)}, s32[64]{0:T(128)}, u32[]{:S(2)}) copy-start(s32[64]{0:T(128)} %param.20) | copy-start | bytes 772
  7.2 104.8 %copy-start.7 = (f32[3,8192]{1,0:T(4,128)S(1)}, f32[3,8192]{1,0:T(4,128)}, u32[]{:S(2)}) copy-start(f32[3,8192]{1,0:T(4,128)} %param.18) | copy-start | bytes 294916
  7.2 104.9 %all-gather.4.cloned.1.call-start = ((), (), s32[]{:S(2)}) async-start(), calls=%async_computation | async-start | bytes 4325376 | tf_op jit(solution)/shard_map/all_gather | solution.py:57
  7.9 795.2 %all-gather.6.cloned.1.call-start = ((), (), s32[]{:S(2)}) async-start(), calls=%async_computation.1 | async-start | bytes 4718592 | tf_op jit(solution)/shard_map/all_gather | solution.py:70
  122.0 2.0 copy-start.1
  439.5 8.5 %copy-start = (f32[1024,1024]{1,0:T(8,128)S(1)}, f32[1024,1024]{1,0:T(8,128)}, u32[]{:S(2)}) copy-start(f32[1024,1024]{1,0:T(8,128)} %get-tuple-element.216) | copy-start | bytes 12582916
  442.7 10.6 %copy-start.9 = (f32[3,128]{1,0:T(4,128)S(1)}, f32[3,128]{1,0:T(4,128)}, u32[]{:S(2)}) copy-start(f32[3,128]{1,0:T(4,128)} %param.15) | copy-start | bytes 4612
  453.4 71.3 %copy-start.2 = (f32[1024,128]{1,0:T(8,128)}, f32[1024,128]{1,0:T(8,128)S(1)}, u32[]{:S(2)}) copy-start(f32[1024,128]{1,0:T(8,128)S(1)} %convolution_dynamic-update-slice_fusion.5) | copy-start | bytes 1572868
  609.0 193.3 %copy-start.5 = (f32[3,8192]{1,0:T(4,128)}, f32[3,8192]{1,0:T(4,128)S(1)}, u32[]{:S(2)}) copy-start(f32[3,8192]{1,0:T(4,128)S(1)} %fusion.270) | copy-start | bytes 294916
  609.0 5.4 collective-permute-start
  612.4 7.0 collective-permute-start.1
  786.3 15.9 %copy-start.4 = (f32[3,6,8192]{2,1,0:T(8,128)S(1)}, f32[3,6,8192]{2,1,0:T(8,128)}, u32[]{:S(2)}) copy-start(f32[3,6,8192]{2,1,0:T(8,128)} %param.21) | copy-start | bytes 1769476
  786.4 16.1 %copy-start.8 = (f32[8192]{0:T(1024)S(1)}, f32[8192]{0:T(1024)}, u32[]{:S(2)}) copy-start(f32[8192]{0:T(1024)} %param.23) | copy-start | bytes 98308
  786.4 16.7 %copy-start.3 = (f32[1024,128]{1,0:T(8,128)S(1)}, f32[1024,128]{1,0:T(8,128)}, u32[]{:S(2)}) copy-start(f32[1024,128]{1,0:T(8,128)} %copy-done.2) | copy-start | bytes 1572868
  786.4 16.7 %copy-start.6 = (f32[128,1024]{1,0:T(8,128)S(1)}, f32[128,1024]{1,0:T(8,128)}, u32[]{:S(2)}) copy-start(f32[128,1024]{1,0:T(8,128)} %param.16) | copy-start | bytes 1572868
Sparse Core Ops, SparseCore 0:
  10.6 54.0 all-gather.3
  524.8 56.4 all-gather.5
where the time goes:
time: 821 us; the launch traced here: 816 us
  other arithmetic  264 us (32%)
  local copies, waits for them, and re-layouts  234 us (29%)
  blocking collectives  159 us (19%)
  matrix products  127 us (15%)
  between operations  19.9 us (2%)
    gather x2, local copies, waits for them, and re-layouts, per_device(): across_disp = extended[:, edge_nbr]  180 us
    another operation x30, other arithmetic, per_device(): factor = jnp.linalg.cholesky(whole_diag)  172 us
    another operation x3, other arithmetic, per_device(): jax.scipy.linalg.solve_triangular(factor, panel_block.T, lower=True)  84.6 us
    dot_general x8, matrix products, slot_term(): jnp.einsum('tnc,atc->atn', kernel, near_weight, precision=highest_mode)  84.3 us
    all_gather x1, blocking collectives, per_device(): lax.all_gather(ctrl_xyz, ('chol', 'vol'), axis=1, tiled=True)  69.3 us
    all_gather x1, blocking collectives, per_device(): lax.all_gather(ctrl_weight, ('chol', 'vol'), axis=1, tiled=True)  65.6 us
    another operation x24, local copies, waits for them, and re-layouts  27.5 us
    all_gather x1, blocking collectives, per_device(): lax.all_gather(rhs_diag, 'vol', axis=1, tiled=True)  24.6 us
  transfers between devices with their start and end apart: 4, of which 1 were waited for; matrix products, arithmetic and copies ran while one was open for 34% of the time, Pallas kernels for 0%

commit v1 on v0

--- a/solution.py
+++ b/solution.py
@@ -6,6 +6,11 @@
 HALO = 128
 highest_mode = lax.Precision.HIGHEST
 support_radius = 1.25
+
+
+def gather_by_exchange(shard, axis, dim):
+    copies = jnp.concatenate([shard] * lax.axis_size(axis), axis=dim)
+    return lax.all_to_all(copies, axis, dim, dim, tiled=True)
 
 
 def with_halo(block, sides, width):
@@ -55,7 +60,7 @@
 ):
     whole_diag, whole_rhs = (
         lax.all_gather(diag_block, "vol", axis=0, tiled=True),
-        lax.all_gather(rhs_diag, "vol", axis=1, tiled=True),
+        gather_by_exchange(rhs_diag, "vol", 1),
     )
     factor = jnp.linalg.cholesky(whole_diag)
     lower_panel = jax.scipy.linalg.solve_triangular(factor, panel_block.T, lower=True).T

time: 821 us -> 818 us (level)
  blocking collectives: 159 us -> 137 us
    all_gather x1 -> x0, blocking collectives: 24.6 us -> none  [per_device(): lax.all_gather(rhs_diag, 'vol', axis=1, tiled=True)]
    another operation x41 -> x24, local copies, waits for them, and re-layouts: 28.3 us -> 29.1 us
  transfers between devices with their start and end apart: 4 -> 5, of which waited for: 1 -> 1; matrix products, arithmetic and copies ran while one was open for 34% -> 34% of each run, Pallas kernels for 0% -> 0%
where the time goes in v1:
time: 818 us; the launch traced here: 812 us
  other arithmetic  264 us (32%)
  local copies, waits for them, and re-layouts  237 us (29%)
  blocking collectives  137 us (17%)
  matrix products  135 us (17%)
  between operations  19.8 us (2%)
  starting transfers between devices  13 us (2%)
    gather x2, local copies, waits for them, and re-layouts, per_device(): across_disp = extended[:, edge_nbr]  181 us
    another operation x30, other arithmetic, per_device(): factor = jnp.linalg.cholesky(whole_diag)  172 us
    another operation x3, other arithmetic, per_device(): jax.scipy.linalg.solve_triangular(factor, panel_block.T, lower=True)  84.6 us
    dot_general x8, matrix products, slot_term(): jnp.einsum('tnc,atc->atn', kernel, near_weight, precision=highest_mode)  84.3 us
    all_gather x1, blocking collectives, per_device(): lax.all_gather(ctrl_xyz, ('chol', 'vol'), axis=1, tiled=True)  71.2 us
    all_gather x1, blocking collectives, per_device(): lax.all_gather(ctrl_weight, ('chol', 'vol'), axis=1, tiled=True)  65.6 us
    another operation x24, local copies, waits for them, and re-layouts  29.1 us
    another operation x14, matrix products, per_device(): factor = jnp.linalg.cholesky(whole_diag)  23.3 us
  transfers between devices with their start and end apart: 5, of which 1 were waited for; matrix products, arithmetic and copies ran while one was open for 34% of the time, Pallas kernels for 0%

profile of v1, /device:TPU:7, one launch (start us, length us, event | category | flops | bytes accessed | tf_op | source)
XLA Modules:
  0.0 812.1 jit_solution(15542167426103059992)
XLA Ops:
  7.9 2.0 concatenate.60
  10.6 7.9 all-to-all-start
  19.6 71.2 %all_gather.15 = f32[3,32768]{1,0:T(4,128)S(1)} all-gather(f32[3,128]{1,0:T(4,128)} %param.17), channel_id=1, replica_groups=mesh['chol'=8,'vol'=32] {'chol','vol'}, dimensions={1}, use_global_device_ids=true | all-gather | bytes 394752 | tf_op jit(solution)/shard_map/all_gather | solution.py:70
  98.0 5.5 copy.47
  103.5 4.4 fusion
  108.0 1.9 copy-done
  109.9 11.7 %cholesky.223 = f32[128,128]{1,0:T(8,128)S(1)} custom-call(f32[128,128]{1,0:T(8,128)S(1)} %cholesky.580), custom_call_target="Cholesky" | custom-call | tf_op jit(solution)/shard_map/jit(cholesky)/cholesky | solution.py:65
  121.7 9.8 %custom-call.66 = f32[1,128,128]{1,2,0:T(8,128)S(1)} custom-call(f32[1,128,128]{2,1,0:T(8,128)S(1)} %get-tuple-element.99), custom_call_target="InvertDiagBlocksLowerTriangular" | custom-call | tf_op jit(solution)/shard_map/jit(cholesky)/cholesky | solution.py:65
  131.5 2.5 cholesky.255
  134.0 2.4 constant_dynamic-update-slice_fusion.57
  136.4 1.5 convolution_subtract_fusion.1
  137.9 11.9 %cholesky.244 = f32[128,128]{1,0:T(8,128)S(1)} custom-call(f32[128,128]{1,0:T(8,128)S(1)} %cholesky.584), custom_call_target="Cholesky" | custom-call | tf_op jit(solution)/shard_map/jit(cholesky)/cholesky | solution.py:65
  150.5 9.8 %custom-call.67 = f32[1,128,128]{1,2,0:T(8,128)S(1)} custom-call(f32[1,128,128]{2,1,0:T(8,128)S(1)} %get-tuple-element.96), custom_call_target="InvertDiagBlocksLowerTriangular" | custom-call | tf_op jit(solution)/shard_map/jit(cholesky)/cholesky | solution.py:65
  161.5 2.1 convolution_subtract_fusion.2
  163.6 11.7 %cholesky.468 = f32[128,128]{1,0:T(8,128)S(1)} custom-call(f32[128,128]{1,0:T(8,128)S(1)} %cholesky.589), custom_call_target="Cholesky" | custom-call | tf_op jit(solution)/shard_map/jit(cholesky)/cholesky | solution.py:65
  176.7 9.8 %custom-call.68 = f32[1,128,128]{1,2,0:T(8,128)S(1)} custom-call(f32[1,128,128]{2,1,0:T(8,128)S(1)} %get-tuple-element.93), custom_call_target="InvertDiagBlocksLowerTriangular" | custom-call | tf_op jit(solution)/shard_map/jit(cholesky)/cholesky | solution.py:65
  187.7 2.3 convolution_subtract_fusion.3
  190.1 12.1 %cholesky.487 = f32[128,128]{1,0:T(8,128)S(1)} custom-call(f32[128,128]{1,0:T(8,128)S(1)} %cholesky.594), custom_call_target="Cholesky" | custom-call | tf_op jit(solution)/shard_map/jit(cholesky)/cholesky | solution.py:65
  203.5 9.8 %custom-call.69 = f32[1,128,128]{1,2,0:T(8,128)S(1)} custom-call(f32[1,128,128]{2,1,0:T(8,128)S(1)} %get-tuple-element.90), custom_call_target="InvertDiagBlocksLowerTriangular" | custom-call | tf_op jit(solution)/shard_map/jit(cholesky)/cholesky | solution.py:65
  214.4 2.4 convolution_subtract_fusion.4
  216.8 11.7 %cholesky.506 = f32[128,128]{1,0:T(8,128)S(1)} custom-call(f32[128,128]{1,0:T(8,128)S(1)} %cholesky.599), custom_call_target="Cholesky" | custom-call | tf_op jit(solution)/shard_map/jit(cholesky)/cholesky | solution.py:65
  229.8 9.9 %custom-call.70 = f32[1,128,128]{1,2,0:T(8,128)S(1)} custom-call(f32[1,128,128]{2,1,0:T(8,128)S(1)} %get-tuple-element.87), custom_call_target="InvertDiagBlocksLowerTriangular" | custom-call | tf_op jit(solution)/shard_map/jit(cholesky)/cholesky | solution.py:65
  240.8 2.3 convolution_subtract_fusion.5
  243.1 11.7 %cholesky.526 = f32[128,128]{1,0:T(8,128)S(1)} custom-call(f32[128,128]{1,0:T(8,128)S(1)} %cholesky.604), custom_call_target="Cholesky" | custom-call | tf_op jit(solution)/shard_map/jit(cholesky)/cholesky | solution.py:65
  256.1 9.8 %custom-call.71 = f32[1,128,128]{1,2,0:T(8,128)S(1)} custom-call(f32[1,128,128]{2,1,0:T(8,128)S(1)} %get-tuple-element.84), custom_call_target="InvertDiagBlocksLowerTriangular" | custom-call | tf_op jit(solution)/shard_map/jit(cholesky)/cholesky | solution.py:65
  266.8 2.0 convolution_subtract_fusion.6
  268.9 11.9 %cholesky.546 = f32[128,128]{1,0:T(8,128)S(1)} custom-call(f32[128,128]{1,0:T(8,128)S(1)} %cholesky.609), custom_call_target="Cholesky" | custom-call | tf_op jit(solution)/shard_map/jit(cholesky)/cholesky | solution.py:65
  282.0 9.8 %custom-call.72 = f32[1,128,128]{1,2,0:T(8,128)S(1)} custom-call(f32[1,128,128]{2,1,0:T(8,128)S(1)} %get-tuple-element.81), custom_call_target="InvertDiagBlocksLowerTriangular" | custom-call | tf_op jit(solution)/shard_map/jit(cholesky)/cholesky | solution.py:65
  292.7 1.9 convolution_subtract_fusion.12
  294.6 11.7 %cholesky.564 = f32[128,128]{1,0:T(8,128)S(1)} custom-call(f32[128,128]{1,0:T(8,128)S(1)} %convolution_subtract_fusion.12), custom_call_target="Cholesky" | custom-call | tf_op jit(solution)/shard_map/jit(cholesky)/cholesky | solution.py:65
  313.2 4.8 select_select_fusion
  318.0 29.1 %while.1 = (s32[]{:T(128)}, f32[1024,1024]{1,0:T(8,128)}, s32[8,2]{0,1:T(2,128)S(1)}, f32[8,128,128]{2,1,0:T(8,128)}, s32[]{:T(128)}) while((s32[]{:T(128)}, f32[1024,1024]{1,0:T(8,128)}, s32[8,2]{0,1:T(2,128)S(1)}, f32[8,128,128]{2,1,0:T(8,128)}, s32[]{:T(128)}) %tuple.121), condition=%wide.while_cond, body=%wide.while_body.sunk | while | flops 2 | bytes 132205 | solution.py:66
  318.7 3.0 bitcast_dynamic-update-slice_fusion.2
  322.3 3.0 bitcast_dynamic-update-slice_fusion.2
  326.0 3.0 bitcast_dynamic-update-slice_fusion.2
  329.6 3.0 bitcast_dynamic-update-slice_fusion.2
  333.3 3.0 bitcast_dynamic-update-slice_fusion.2
  336.9 3.0 bitcast_dynamic-update-slice_fusion.2
  340.6 3.0 bitcast_dynamic-update-slice_fusion.2
  344.2 2.9 bitcast_dynamic-update-slice_fusion.2
  347.1 79.8 %custom-call.73 = f32[8,128,128]{1,2,0:T(8,128)S(1)} custom-call(f32[8,128,128]{2,1,0:T(8,128)} %get-tuple-element.10), custom_call_target="InvertDiagBlocksLowerTriangular" | custom-call | tf_op jit(solution)/shard_map/jit(_solve_triangular)/triangular_solve | solution.py:66
  432.5 1.4 convolution_subtract_fusion.16
  434.1 1.4 convolution_subtract_fusion.22
  435.7 1.5 convolution_subtract_fusion.15
  441.9 1.3 convolution_subtract_fusion.13
  443.5 1.4 convolution_subtract_fusion.9
  445.3 1.5 convolution_subtract_fusion.8
  447.1 1.6 convolution_subtract_fusion.7
  449.5 65.6 %all_gather.14 = f32[3,32768]{1,0:T(4,128)S(1)} all-gather(f32[3,128]{1,0:T(4,128)S(1)} %convolution_subtract_fusion.21), channel_id=1, replica_groups=mesh['chol'=8,'vol'=32] {'chol','vol'}, dimensions={1}, use_global_device_ids=true | all-gather | bytes 394752 | tf_op jit(solution)/shard_map/all_gather | solution.py:71
  520.5 10.7 %fusion.231 = f32[64,3,128]{2,1,0:T(4,128)S(1)} fusion(f32[64,128]{1,0:T(8,128)S(1)} %bitcast.325, f32[64,128]{1,0:T(8,128)S(1)} %bitcast.324, f32[64,128]{1,0:T(8,128)S(1)} %bitcast.323, f32[64,128]{1,0:T(8,128)S(1)} %bitcast.295, f32[64,128]{1,0:T(8,128)S(1)} %bitcast.303, f32[64,128]{1,0:T(8,128)S(1)} %bitcast.287, f32[64,3,128]{2,1,0:T(4,128)S(1)} %gather_fusion.2, ...), kind=kOutput, calls=%fused_computation.261 | convolution fusion | flops 54550528 | bytes 393472 | tf_op jit(solution)/shard_map/tnc,atc->atn/dot_general | solution.py:43
  531.1 10.5 %fusion.228 = f32[64,3,128]{2,1,0:T(4,128)S(1)} fusion(f32[64,3,128]{2,1,0:T(4,128)S(1)} %fusion.231, f32[64,128]{1,0:T(8,128)S(1)} %bitcast.322, f32[64,128]{1,0:T(8,128)S(1)} %bitcast.296, f32[64,128]{1,0:T(8,128)S(1)} %bitcast.321, f32[64,128]{1,0:T(8,128)S(1)} %bitcast.304, f32[64,128]{1,0:T(8,128)S(1)} %bitcast.320, f32[64,128]{1,0:T(8,128)S(1)} %bitcast.288, ...), kind=kOutput, calls=%fused_computation.260 | convolution fusion | flops 54575104 | bytes 491776 | tf_op jit(solution)/shard_map/tnc,atc->atn/dot_general | solution.py:43
  541.7 10.5 %fusion.237 = f32[64,3,128]{2,1,0:T(4,128)S(1)} fusion(f32[64,3,128]{2,1,0:T(4,128)S(1)} %fusion.228, f32[64,128]{1,0:T(8,128)S(1)} %bitcast.319, f32[64,128]{1,0:T(8,128)S(1)} %bitcast.318, f32[64,128]{1,0:T(8,128)S(1)} %bitcast.317, f32[64,128]{1,0:T(8,128)S(1)} %bitcast.297, f32[64,128]{1,0:T(8,128)S(1)} %bitcast.305, f32[64,128]{1,0:T(8,128)S(1)} %bitcast.289, ...), kind=kOutput, calls=%fused_computation.263 | convolution fusion | flops 54575104 | bytes 491776 | tf_op jit(solution)/shard_map/tnc,atc->atn/dot_general | solution.py:43
  552.2 10.5 %fusion.243 = f32[64,3,128]{2,1,0:T(4,128)S(1)} fusion(f32[64,3,128]{2,1,0:T(4,128)S(1)} %fusion.237, f32[64,128]{1,0:T(8,128)S(1)} %bitcast.316, f32[64,128]{1,0:T(8,128)S(1)} %bitcast.315, f32[64,128]{1,0:T(8,128)S(1)} %bitcast.314, f32[64,128]{1,0:T(8,128)S(1)} %bitcast.298, f32[64,128]{1,0:T(8,128)S(1)} %bitcast.306, f32[64,128]{1,0:T(8,128)S(1)} %bitcast.290, ...), kind=kOutput, calls=%fused_computation.265 | convolution fusion | flops 54575104 | bytes 491776 | tf_op jit(solution)/shard_map/tnc,atc->atn/dot_general | solution.py:43
  562.7 10.5 %fusion.249 = f32[64,3,128]{2,1,0:T(4,128)S(1)} fusion(f32[64,3,128]{2,1,0:T(4,128)S(1)} %fusion.243, f32[64,128]{1,0:T(8,128)S(1)} %bitcast.313, f32[64,128]{1,0:T(8,128)S(1)} %bitcast.312, f32[64,128]{1,0:T(8,128)S(1)} %bitcast.311, f32[64,128]{1,0:T(8,128)S(1)} %bitcast.299, f32[64,128]{1,0:T(8,128)S(1)} %bitcast.307, f32[64,128]{1,0:T(8,128)S(1)} %bitcast.291, ...), kind=kOutput, calls=%fused_computation.267 | convolution fusion | flops 54575104 | bytes 491776 | tf_op jit(solution)/shard_map/tnc,atc->atn/dot_general | solution.py:43
  573.2 10.5 %fusion.255 = f32[64,3,128]{2,1,0:T(4,128)S(1)} fusion(f32[64,3,128]{2,1,0:T(4,128)S(1)} %fusion.249, f32[64,128]{1,0:T(8,128)S(1)} %bitcast.286, f32[64,128]{1,0:T(8,128)S(1)} %bitcast.285, f32[64,128]{1,0:T(8,128)S(1)} %bitcast.284, f32[64,128]{1,0:T(8,128)S(1)} %bitcast.300, f32[64,128]{1,0:T(8,128)S(1)} %bitcast.308, f32[64,128]{1,0:T(8,128)S(1)} %bitcast.292, ...), kind=kOutput, calls=%fused_computation.269 | convolution fusion | flops 54575104 | bytes 491776 | tf_op jit(solution)/shard_map/tnc,atc->atn/dot_general | solution.py:43
  583.7 10.5 %fusion.261 = f32[64,3,128]{2,1,0:T(4,128)S(1)} fusion(f32[64,3,128]{2,1,0:T(4,128)S(1)} %fusion.255, f32[64,128]{1,0:T(8,128)S(1)} %bitcast.283, f32[64,128]{1,0:T(8,128)S(1)} %bitcast.282, f32[64,128]{1,0:T(8,128)S(1)} %bitcast.281, f32[64,128]{1,0:T(8,128)S(1)} %bitcast.301, f32[64,128]{1,0:T(8,128)S(1)} %bitcast.309, f32[64,128]{1,0:T(8,128)S(1)} %bitcast.293, ...), kind=kOutput, calls=%fused_computation.271 | convolution fusion | flops 54575104 | bytes 491776 | tf_op jit(solution)/shard_map/tnc,atc->atn/dot_general | solution.py:43
  594.2 10.5 %fusion.270 = f32[3,8192]{1,0:T(4,128)S(1)} fusion(f32[64,3,128]{2,1,0:T(4,128)S(1)} %fusion.261, f32[64,128]{1,0:T(8,128)S(1)} %bitcast.280, f32[64,128]{1,0:T(8,128)S(1)} %bitcast.279, f32[64,128]{1,0:T(8,128)S(1)} %bitcast.278, f32[64,128]{1,0:T(8,128)S(1)} %bitcast.302, f32[64,128]{1,0:T(8,128)S(1)} %bitcast.310, f32[64,128]{1,0:T(8,128)S(1)} %bitcast.294, ...), kind=kOutput, calls=%fused_computation.274 | convolution fusion | flops 54575104 | bytes 491776 | tf_op jit(solution)/shard_map/tnc,atc->atn/dot_general | solution.py:43
  604.8 3.1 collective-permute-start
  607.9 1.9 collective-permute-start.1
  609.9 5.0 collective-permute-done.1
  615.0 2.7 copy.59
  617.7 165.3 %gather_fusion.16 = f32[49152,3]{1,0:T(8,128)} fusion(f32[3,8448]{0,1:T(8,128)} %copy.59, s32[49152]{0:T(1024)S(1)} %broadcast_clamp_fusion), kind=kCustom, calls=%fused_computation.16 | custom fusion | bytes 1376256 | tf_op jit(solution)/shard_map/gather | solution.py:92
  783.0 15.9 %copy.60 = f32[6,8192,3]{1,0,2:T(8,128)S(1)} copy(f32[6,8192,3]{2,1,0:T(8,128)} %bitcast.236) | data formatting | bytes 1179648 | tf_op jit(solution)/shard_map/gather | solution.py:92
  799.7 5.4 convolution_subtract_fusion
  (143 shorter events, 49.0 us)
Async XLA Ops:
  7.2 90.2 %copy-start.8 = (f32[3,8192]{1,0:T(4,128)S(1)}, f32[3,8192]{1,0:T(4,128)}, u32[]{:S(2)}) copy-start(f32[3,8192]{1,0:T(4,128)} %param.18) | copy-start | bytes 294916
  7.2 90.3 %copy-start.7 = (s32[6,8192]{1,0:T(8,128)S(1)}, s32[6,8192]{1,0:T(8,128)}, u32[]{:S(2)}) copy-start(s32[6,8192]{1,0:T(8,128)} %param.22) | copy-start | bytes 589828
  7.2 90.5 %copy-start.5 = (f32[128,1024]{1,0:T(8,128)S(1)}, f32[128,1024]{1,0:T(8,128)}, u32[]{:S(2)}) copy-start(f32[128,1024]{1,0:T(8,128)} %param.14) | copy-start | bytes 1572868
  7.2 90.8 %all-gather.3.cloned.1.call-start = ((), (), s32[]{:S(2)}) async-start(), calls=%async_computation.1 | async-start | bytes 4325376 | tf_op jit(solution)/shard_map/all_gather | solution.py:62
  10.6 87.2 %all-to-all-start = ((f32[3,32,32]{2,0,1:T(4,128)}), f32[3,32,32]{2,0,1:T(4,128)S(1)}, u32[]{:S(2)}, u32[]{:S(2)}) async-start(f32[3,32,32]{2,0,1:T(4,128)} %copy.49), calls=%async_computation | async-start | bytes 131072 | tf_op jit(solution)/shard_map/all_to_all | solution.py:13
  18.5 781.2 %all-gather.5.cloned.1.call-start = ((), (), s32[]{:S(2)}) async-start(), calls=%async_computation.2 | async-start | bytes 4718592 | tf_op jit(solution)/shard_map/all_gather | solution.py:75
  108.0 2.0 copy-start
  435.5 13.6 %copy-start.10 = (f32[3,128]{1,0:T(4,128)S(1)}, f32[3,128]{1,0:T(4,128)}, u32[]{:S(2)}) copy-start(f32[3,128]{1,0:T(4,128)} %param.15) | copy-start | bytes 4612
  449.1 71.3 %copy-start.1 = (f32[1024,128]{1,0:T(8,128)}, f32[1024,128]{1,0:T(8,128)S(1)}, u32[]{:S(2)}) copy-start(f32[1024,128]{1,0:T(8,128)S(1)} %convolution_dynamic-update-slice_fusion.5) | copy-start | bytes 1572868
  604.7 194.1 %copy-start.4 = (f32[3,8192]{1,0:T(4,128)}, f32[3,8192]{1,0:T(4,128)S(1)}, u32[]{:S(2)}) copy-start(f32[3,8192]{1,0:T(4,128)S(1)} %fusion.270) | copy-start | bytes 294916
  604.8 5.1 collective-permute-start
  607.9 7.0 collective-permute-start.1
  783.0 15.9 %copy-start.3 = (f32[3,6,8192]{2,1,0:T(8,128)S(1)}, f32[3,6,8192]{2,1,0:T(8,128)}, u32[]{:S(2)}) copy-start(f32[3,6,8192]{2,1,0:T(8,128)} %param.21) | copy-start | bytes 1769476
  783.0 16.1 %copy-start.9 = (f32[8192]{0:T(1024)S(1)}, f32[8192]{0:T(1024)}, u32[]{:S(2)}) copy-start(f32[8192]{0:T(1024)} %param.23) | copy-start | bytes 98308
  783.0 16.7 %copy-start.2 = (f32[1024,128]{1,0:T(8,128)S(1)}, f32[1024,128]{1,0:T(8,128)}, u32[]{:S(2)}) copy-start(f32[1024,128]{1,0:T(8,128)} %copy-done.1) | copy-start | bytes 1572868
  783.0 16.7 %copy-start.6 = (f32[128,1024]{1,0:T(8,128)S(1)}, f32[128,1024]{1,0:T(8,128)}, u32[]{:S(2)}) copy-start(f32[128,1024]{1,0:T(8,128)} %param.16) | copy-start | bytes 1572868
Sparse Core Ops, SparseCore 0:
  10.6 54.0 all-gather.2
  520.6 56.2 all-gather.4
